TPU v7x, 128 devices: a whole 4x4x4 slice. The times are simulated.
128 devices in a mesh: section: 8 (over x, y_hi), head: 8 (over z, y_lo), batch: 2 (over core).
Axes of the slice: x: 4, y: 4 (y_hi: 2, y_lo: 2; y = y_hi * 2 + y_lo), z: 4, core: 2. Of those that a mesh axis runs over, the one named last changes fastest.
Arguments:
- keys_prefill: bfloat16 [8, 32, 512, 1024], P('section', 'batch', None, 'head'), may hold values from -6 to 6
- values_prefill: bfloat16 [8, 32, 512, 1024], P('section', 'batch', None, 'head'), may hold values from -6 to 6
- lengths: int32 [32], replicated, may hold values from 1 to 510, 8192 in all
- slot_order: int32 [32], replicated, may hold values from 0 to 31, each once
- queries: bfloat16 [2, 8, 32, 8192], P(None, None, 'section'), may hold values from -51 to 51
- new_keys: bfloat16 [2, 8, 32, 1024], P(None, None, 'section'), may hold values from -5 to 5
- new_values: bfloat16 [2, 8, 32, 1024], P(None, None, 'section'), may hold values from -6 to 6
Outputs:
- attention: bfloat16 [2, 8, 32, 8192], P(None, None, 'section', ('head', 'batch'))
- keys_cache: bfloat16 [8, 32, 512, 1024], P(None, 'section', ('head', 'batch'))
- values_cache: bfloat16 [8, 32, 512, 1024], P(None, 'section', ('head', 'batch'))
Inputs may be any that keep to these rules, and one draw needn't show every extreme that they name: lengths[p] is the number of cached tokens of prompt p; the prefill cache holds stale values from position lengths[p] on, which are not part of the cache (zero in keys_cache and values_cache unless a new row is placed there, and never visible to attention). `slot_order`: each prompt appears in exactly one decode slot.
All inputs are finite; a program needn't handle non-finite values.
Results may differ from a plain program's by a relative error of at most 0.0044.
Values may be sent and summed in bfloat16 or wider, within the bound.
A program may use at most 128 MiB of HBM per device.

v0:
```python
import jax
import jax.numpy as jnp
from jax import lax
from jax.experimental import pallas as pl
from jax.experimental.pallas import tpu as pltpu
from jax.sharding import PartitionSpec as P

KVH = 8
HD = 128
GROUP = 8
BLOCK = 32
MESH = pl.DeviceIdType.MESH
HIDDEN = -1e30
BF16, F32 = jnp.bfloat16, jnp.float32


PLANE = {
    1: ((1, 1), (3, 3), (1, 3), (3, 1), (2, 1), (0, 3), (2, 3), (0, 1)),
    0: ((1, 0), (0, 2), (3, 2), (1, 2), (3, 0), (2, 2), (2, 0)),
}
ARRIVALS = {low: tuple((dx, low) for dx in (1, 3, 2, 0)) for low in (1, 0)}


def group_of(dx, low):
    return low * 4 + dx


def relay(
    slot_order_hbm, lengths_hbm, keys, values, queries, new_keys, new_values,
    attention, keys_cache, values_cache,
    full, keys_line, values_chip, keys_packed, values_packed, keys_land, values_mid, values_land,
    fresh_rows, query_all, query_rows, fresh_all, rows_send, rows_land,
    slot_order, lengths,
    scalar_sem, full_sem, fresh_sem, line_send, line_recv, chip_send, chip_recv,
    keys_send, keys_recv, mid_send, mid_recv, values_send, values_recv,
    small_send, small_recv, rows_send_sem, rows_recv_sem,
):
    s, h, b = lax.axis_index("section"), lax.axis_index("head"), lax.axis_index("batch")
    x, z = lax.div(s, 2), lax.div(h, 2)
    y_low = lax.rem(h, 2)
    y = lax.rem(s, 2) * 2 + y_low
    other = 1 - b
    sign = 1 - 2 * b
    mine = pl.ds(b * 16, 16)
    here = x * 4 + y
    here_mid = x * 4 + y_low * 2 + lax.div(y, 2)

    def remote(src, dst, send_sem, recv_sem, to):
        return pltpu.make_async_remote_copy(
            src_ref=src, dst_ref=dst, send_sem=send_sem, recv_sem=recv_sem,
            device_id=to, device_id_type=MESH,
        )

    def wait_for(ref, sem):
        pltpu.make_async_copy(ref, ref, sem).wait()

    def away(d, at, way):
        return lax.rem(at + way * d + 4, 4)

    def in_plane(at_x, at_y):
        return at_x * 2 + lax.div(at_y, 2), z * 2 + lax.rem(at_y, 2)

    def in_line(at_z):
        return at_z * 2 + y_low

    def owner_low(low):
        return lax.rem(y_low + low, 2)

    barrier = pltpu.get_barrier_semaphore()

    def greet(to):
        pl.semaphore_signal(barrier, inc=1, device_id=to, device_id_type=MESH)

    for dz in range(4):
        at_h = in_line(away(dz, z, 1))
        greet((s, at_h, other))
        if dz:
            greet((s, at_h, b))
    for low in (1, 0):
        for dx, dy in PLANE[low]:
            at_s, at_h = in_plane(away(dx, x, 1), away(dy, y, 1))
            greet((at_s, at_h, b))
            if low == 0:
                greet((at_s, at_h, other))

    scalars = [
        pltpu.make_async_copy(slot_order_hbm, slot_order, scalar_sem.at[0]),
        pltpu.make_async_copy(lengths_hbm, lengths, scalar_sem.at[1]),
    ]
    whole = [pltpu.make_async_copy(src, full.at[n], full_sem.at[n]) for n, src in enumerate((keys, values))]
    fresh = [
        pltpu.make_async_copy(src, fresh_rows.at[n], fresh_sem.at[n])
        for n, src in enumerate((new_keys, new_values))
    ]
    for copy in scalars:
        copy.start()
    for low in (1, 0):
        pltpu.make_async_copy(
            values.at[:, :, owner_low(low), b], values_chip[low].at[mine], chip_recv.at[low]
        ).start()
    for low in (1, 0):
        pltpu.make_async_copy(
            keys.at[:, z, owner_low(low), b], keys_line[low].at[z, mine], line_recv.at[low]
        ).start()
    for copy in whole + fresh:
        copy.start()
    pl.semaphore_wait(barrier, 29)

    for low in (1, 0):
        remote(
            values.at[:, :, owner_low(low), other], values_chip[low].at[mine],
            chip_send, chip_recv.at[low], (s, h, other),
        ).start()

    def send_line(low, dz, to_b):
        to_z = away(dz, z, sign)
        remote(
            keys.at[:, to_z, owner_low(low), to_b], keys_line[low].at[z, mine],
            line_send, line_recv.at[low], (s, in_line(to_z), to_b),
        ).start()

    lines = [
        (low, dz, to_b)
        for low in (1, 0)
        for dz, to_b in ((1, b), (3, other), (2, b), (1, other), (3, b), (2, other), (0, other))
    ]
    for line in lines[:3]:
        send_line(*line)

    head_rows = pl.ds(pl.multiple_of(h * GROUP * HD, GROUP * HD), GROUP * HD)
    head_cols = pl.ds(pl.multiple_of(h * HD, HD), HD)

    def small_pieces(to_s):
        return (
            (queries.at[:, to_s, :, head_rows], query_all.at[s]),
            (new_keys.at[:, to_s, :, head_cols], fresh_all.at[0, s]),
            (new_values.at[:, to_s, :, head_cols], fresh_all.at[1, s]),
        )

    def send_small(step, carry):
        to_s = lax.rem(s + step, 8)
        for n, (src, dst) in enumerate(small_pieces(to_s)):
            remote(src, dst, small_send.at[n], small_recv.at[n], (to_s, h, b)).start()
        return carry

    lax.fori_loop(1, 8, send_small, 0)
    for n, (src, dst) in enumerate(small_pieces(s)):
        pltpu.make_async_copy(src, dst, small_recv.at[n]).start()

    scalars[0].wait()
    scalars[1].wait()

    def pack_values(low):
        def step(at_s, carry):
            for k in range(4):
                values_packed[at_s * 2 + owner_low(low), :, k] = values_chip[low][slot_order[at_s * 4 + k]]
            return carry

        lax.fori_loop(0, 8, step, 0)

    def pack_keys(low):
        def step(at_s, carry):
            for k in range(4):
                slot = slot_order[at_s * 4 + k]
                for from_z in range(4):
                    keys_packed[at_s * 2 + owner_low(low), from_z, k] = keys_line[low][from_z, slot]
            return carry

        lax.fori_loop(0, 8, step, 0)

    def send_plane(packed, dx, dy, dst, send_sem, recv_sem):
        to_x, to_y = away(dx, x, sign), away(dy, y, sign)
        to_s, to_h = in_plane(to_x, to_y)
        remote(
            packed.at[to_x * 4 + to_y], dst, send_sem, recv_sem.at[group_of(dx, dy % 2)], (to_s, to_h, b)
        ).start()

    lines = lines[3:]
    for low in (1, 0):
        wait_for(values_chip[low], chip_recv.at[low])
        pack_values(low)
        for dx, dy in PLANE[low]:
            send_plane(values_packed, dx, dy, values_mid.at[:, here_mid], mid_send, mid_recv)
            if lines:
                send_line(*lines.pop(0))
    assert not lines
    pltpu.make_async_copy(
        values_packed.at[here], values_mid.at[:, here_mid], mid_recv.at[group_of(0, 0)]
    ).start()

    def start_of(dx, low):
        return away(dx, x, -sign) * 4 + owner_low(low) * 2

    def turn_keys(low):
        wait_for(keys_line[low], line_recv.at[low])
        pack_keys(low)
        for dx, dy in PLANE[low]:
            send_plane(keys_packed, dx, dy, keys_land.at[here], keys_send, keys_recv)

    def turn_values(low):
        for dx, low in ARRIVALS[low]:
            group = group_of(dx, low)
            wait_for(values_mid.at[:, pl.ds(0, 2)], mid_recv.at[group])
            pair = pl.ds(start_of(dx, low), 2)
            for dz in (1, 3, 2):
                to_z = away(dz, z, sign)
                remote(
                    values_mid.at[to_z, pair], values_land.at[z, pair],
                    values_send, values_recv.at[group], (s, in_line(to_z), b),
                ).start()

    for n, part in enumerate((query_all, fresh_all.at[0], fresh_all.at[1])):
        wait_for(part, small_recv.at[n])
    whole[0].wait()
    whole[1].wait()

    later = lax.rem(lax.div(lax.broadcasted_iota(jnp.int32, (16, 1), 0), 4), 2) == 1
    column = lax.broadcasted_iota(jnp.int32, (16, 512), 1)
    scale = HD ** -0.5

    def attend(at_s, at_k):
        slot = slot_order[at_s * 4 + at_k]
        prompt = slot - b * 16
        inside = jnp.logical_and(prompt >= 0, prompt < 16)
        prompt = jnp.clip(prompt, 0, 15)
        live = lengths[slot]
        qf = query_rows[at_k]
        k0, k1, v0, v1 = (
            fresh_all[n, at_s, t].astype(F32)[at_k : at_k + 1] for n in range(2) for t in range(2)
        )
        k = full[0, prompt].reshape(512, HD)
        v = full[1, prompt].reshape(512, HD)
        scores = lax.dot_general(
            qf.astype(BF16), k, (((1,), (1,)), ((), ())), preferred_element_type=F32
        ) * scale
        n0 = jnp.sum(qf * k0, axis=1, keepdims=True) * scale
        n1 = jnp.sum(qf * k1, axis=1, keepdims=True) * scale
        kept = column < live
        scores = jnp.where(kept, scores, HIDDEN)
        n1 = jnp.where(later, n1, HIDDEN)
        peak = jnp.maximum(jnp.max(scores, axis=1, keepdims=True), jnp.maximum(n0, n1))
        mass = jnp.where(kept, jnp.exp(scores - peak), 0.0)
        m0 = jnp.exp(n0 - peak)
        m1 = jnp.where(later, jnp.exp(n1 - peak), 0.0)
        total = jnp.sum(mass, axis=1, keepdims=True) + m0 + m1
        weighted = jnp.dot(mass.astype(BF16), v, preferred_element_type=F32)
        weighted += m0.astype(BF16).astype(F32) * v0
        weighted += m1.astype(BF16).astype(F32) * v1
        return jnp.where(inside, weighted / total, 0.0)

    def attend_section(at_s, carry):
        for t in range(2):
            rows = query_all[at_s, t].astype(F32)
            for g in range(GROUP):
                row = (g // 4) * 8 + t * 4 + g % 4
                for k in range(4):
                    query_rows[k, row : row + 1, :] = rows[k : k + 1, g * HD : g * HD + HD]
        for pair in range(2):
            first, second = attend(at_s, pair * 2), attend(at_s, pair * 2 + 1)
            for to_b in range(2):
                cut = slice(to_b * 8, to_b * 8 + 8)
                rows_send[at_s, to_b, pair] = jnp.concatenate(
                    (first[cut], second[cut]), axis=0
                ).astype(BF16)
        return carry

    lax.fori_loop(0, 4, attend_section, 0)
    turn_keys(1)
    turn_values(1)
    lax.fori_loop(4, 8, attend_section, 0)

    def send_rows(to_s, to_b):
        remote(
            rows_send.at[to_s, to_b], rows_land.at[s, b], rows_send_sem, rows_recv_sem, (to_s, h, to_b)
        ).start()

    def send_rows_step(step, carry):
        to_s = lax.rem(s + step, 8)
        send_rows(to_s, b)
        send_rows(to_s, other)
        return carry

    lax.fori_loop(1, 8, send_rows_step, 0)
    send_rows(s, other)
    pltpu.make_async_copy(rows_send.at[s, b], rows_land.at[s, b], rows_recv_sem).start()
    turn_keys(0)
    turn_values(0)

    slots = [slot_order[s * 4 + k] for k in range(4)]
    lives = [lengths[slot] for slot in slots]
    position = (h * 2 + b) * BLOCK + lax.broadcasted_iota(jnp.int32, (BLOCK, HD), 0)
    fresh[0].wait()
    fresh[1].wait()

    def settle(block, n, from_x, from_y, from_z):
        layer = from_x * 2 + lax.div(from_y, 2)
        cut = pl.ds(pl.multiple_of((from_z * 2 + lax.rem(from_y, 2)) * HD, HD), HD)
        out = (keys_cache, values_cache)[n]
        placed = [fresh_rows[n, t, layer, :, cut].astype(F32) for t in range(2)]
        for k in range(4):
            rows = jnp.where(position < lives[k], block[k].astype(F32), 0.0)
            for t in range(2):
                rows = jnp.where(position == lives[k] + t, placed[t][k : k + 1], rows)
            out[layer, k, :, cut] = rows.astype(BF16)

    def settle_keys(src, from_x, from_y):
        def step(from_z, carry):
            settle(src.at[from_x * 4 + from_y, from_z], 0, from_x, from_y, from_z)
            return carry

        lax.fori_loop(0, 4, step, 0)

    def settle_values(src, from_x, low, from_z):
        def step(half, carry):
            from_low = owner_low(low)
            block = src.at[from_z, from_x * 4 + from_low * 2 + half]
            settle(block, 1, from_x, half * 2 + from_low, from_z)
            return carry

        lax.fori_loop(0, 2, step, 0)

    owners = [lax.div(slot, 16) for slot in slots]

    def assemble(l, carry):
        picked = []
        for k in range(4):
            part = slice((k % 2) * 8, (k % 2) * 8 + 8)
            first, second = (rows_land[l, n, k // 2].astype(F32)[part] for n in range(2))
            picked.append(jnp.where(owners[k] == 0, first, second))
        for t in range(2):
            attention[t, l] = jnp.concatenate(
                [
                    jnp.concatenate([rows[t * 4 + g : t * 4 + g + 1] for rows in picked], axis=0)
                    for g in range(4)
                ],
                axis=1,
            ).astype(BF16)
        return carry

    settle_keys(keys_packed, x, y)
    for low in (1, 0):
        for dx, _ in ARRIVALS[low]:
            settle_values(values_mid, away(dx, x, -sign), low, z)
    for low in (1, 0):
        if low == 0:
            wait_for(rows_land, rows_recv_sem)
            lax.fori_loop(0, 8, assemble, 0)
        for dx, _ in ARRIVALS[low]:
            group = group_of(dx, low)
            from_x = away(dx, x, -sign)
            chips = [dy for to_x, dy in PLANE[low] if to_x == dx]
            wait_for(keys_land.at[pl.ds(0, len(chips))], keys_recv.at[group])
            for dy in chips:
                settle_keys(keys_land, from_x, away(dy, y, -sign))
            wait_for(values_land.at[pl.ds(0, 3), pl.ds(0, 2)], values_recv.at[group])
            for dz in (1, 3, 2):
                settle_values(values_land, from_x, low, away(dz, z, -sign))

    half = full.at[0, :, pl.ds(0, 2)]
    wait_for(half, chip_send)
    wait_for(half, line_send)
    wait_for(full.at[0, :, pl.ds(2, 1)], line_send)
    wait_for(full.at[0, :, pl.ds(3, 1), pl.ds(0, 1)], line_send)
    for n, part in enumerate((query_all, fresh_all.at[0], fresh_all.at[1])):
        wait_for(part.at[pl.ds(0, 7)], small_send.at[n])
    wait_for(values_packed.at[pl.ds(0, 15)], mid_send)
    wait_for(keys_packed.at[pl.ds(0, 15)], keys_send)
    wait_for(values_land.at[pl.ds(0, 3)], values_send)
    wait_for(rows_send.at[pl.ds(0, 7)], rows_send_sem)
    wait_for(rows_send.at[0, 0], rows_send_sem)


def hand_out(attention, keys, values, attention_out, keys_out, values_out, sem):
    copies = [pltpu.make_async_copy(attention, attention_out, sem.at[16])]
    for n, (src, dst) in enumerate(((keys, keys_out), (values, values_out))):
        copies += [pltpu.make_async_copy(src.at[l], dst.at[l], sem.at[n * 8 + l]) for l in range(8)]
    for copy in copies:
        copy.start()
    for copy in copies:
        copy.wait()


def body(keys_prefill, values_prefill, lengths, slot_order, queries, new_keys, new_values):
    keys = keys_prefill.reshape(16, 4, 2, 2, BLOCK, HD)
    values = values_prefill.reshape(16, 4, 2, 2, BLOCK, HD)
    any_spec = pl.BlockSpec(memory_space=pl.ANY)
    hbm_spec = pl.BlockSpec(memory_space=pltpu.HBM)
    vmem_spec = pl.BlockSpec(memory_space=pltpu.VMEM)
    dma, vmem = pltpu.SemaphoreType.DMA, pltpu.VMEM
    rows_shape, cache_shape = (2, 8, 4, 4 * HD), (8, 4, BLOCK, KVH * HD)
    plane, line = vmem((16, 4, 4, BLOCK, HD), BF16), vmem((4, 16, 4, BLOCK, HD), BF16)

    def in_hbm(array):
        return pltpu.with_memory_space_constraint(array, pltpu.HBM)

    held = pl.pallas_call(
        relay,
        out_shape=(vmem(rows_shape, BF16), vmem(cache_shape, BF16), vmem(cache_shape, BF16)),
        in_specs=[hbm_spec] * 7,
        out_specs=(vmem_spec,) * 3,
        scratch_shapes=[
            vmem((2, 16, 4, 2, 2, BLOCK, HD), BF16),
            [vmem((4, 32, BLOCK, HD), BF16)] * 2, [vmem((32, 4, BLOCK, HD), BF16)] * 2,
            plane, plane, plane, line, line,
            vmem((2, 2, 8, 4, KVH * HD), BF16), vmem((8, 2, 4, GROUP * HD), BF16), vmem((4, 16, HD), F32),
            vmem((2, 8, 2, 4, HD), BF16),
            vmem((8, 2, 2, 16, HD), BF16), vmem((8, 2, 2, 16, HD), BF16),
            pltpu.SMEM((32,), jnp.int32), pltpu.SMEM((32,), jnp.int32),
            dma((2,)), dma((2,)), dma((2,)), dma, dma((2,)), dma, dma((2,)),
            dma, dma((8,)), dma, dma((8,)), dma, dma((8,)),
            dma((3,)), dma((3,)), dma, dma,
        ],
        compiler_params=pltpu.CompilerParams(
            collective_id=0, has_side_effects=True, vmem_limit_bytes=48 * 2**20
        ),
        name="relay",
    )(*(in_hbm(x) for x in (slot_order, lengths, keys, values, queries, new_keys, new_values)))
    return pl.pallas_call(
        hand_out,
        out_shape=tuple(jax.ShapeDtypeStruct(shape, BF16) for shape in (rows_shape, cache_shape, cache_shape)),
        in_specs=[vmem_spec] * 3,
        out_specs=(any_spec,) * 3,
        scratch_shapes=[dma((17,))],
        compiler_params=pltpu.CompilerParams(vmem_limit_bytes=8 * 2**20),
        name="hand_out",
    )(*(pltpu.with_memory_space_constraint(x, pltpu.VMEM) for x in held))


def solution(mesh):
    in_specs = (
        P("section", "batch", None, "head"),
        P("section", "batch", None, "head"),
        P(),
        P(),
        P(None, None, "section", None),
        P(None, None, "section", None),
        P(None, None, "section", None),
    )
    out_specs = (
        P(None, None, "section", ("head", "batch")),
        P(None, "section", ("head", "batch"), None),
        P(None, "section", ("head", "batch"), None),
    )
    return jax.shard_map(body, mesh=mesh, in_specs=in_specs, out_specs=out_specs, check_vma=False)
```

profile of v0, /device:TPU:1, one launch (start us, length us, event | category | flops | bytes accessed | tf_op | source)
XLA Modules:
  0.0 63.2 jit_solution(7400052006325935172)
XLA Ops:
  0.6 60.4 %relay.1 = (bf16[2,8,4,512]{3,2,1,0:T(4,128)(2,1)S(1)}, bf16[8,4,32,1024]{3,2,1,0:T(8,128)(2,1)S(1)}, bf16[8,4,32,1024]{3,2,1,0:T(8,128)(2,1)S(1)}) custom-call(s32[32]{0:T(128)} %slot_order_hbm.1, s32[32]{0:T(128)} %lengths_hbm.1, bf16[16,4,2,2,32,128]{5,4,3,2,1,0:T(8,128)(2,1)} %bitcast.2, bf16[16,4,2,2,32,128]{5,4,3,2,1,0:T(8,128)(2,1)} %bitcast.3, ...), custom_call_target="tpu_custom_call" | custom-call | tf_op jit(solution)/shard_map/relay/pallas_call | solution.py:396
  61.1 2.2 %hand_out.1 = (bf16[2,8,4,512]{3,2,1,0:T(4,128)(2,1)}, bf16[8,4,32,1024]{3,2,1,0:T(8,128)(2,1)}, bf16[8,4,32,1024]{3,2,1,0:T(8,128)(2,1)}) custom-call(bf16[2,8,4,512]{3,2,1,0:T(4,128)(2,1)S(1)} %get-tuple-element.6.attention, bf16[8,4,32,1024]{3,2,1,0:T(8,128)(2,1)S(1)} %get-tuple-element.7.keys, bf16[8,4,32,1024]{3,2,1,0:T(8,128)(2,1)S(1)} %get-tuple-element.8.values), custom_call_target="tpu_custom_call" | custom-call | tf_op jit(solution)/shard_map/hand_out/pallas_call | solution.py:418
where the time goes:
time: 63.3 us; the launch traced here: 63.2 us
  Pallas kernels  62.6 us (99%)
  between operations  0.64 us (1%)
    pallas_call x1, Pallas kernels, body(): pl.pallas_call(relay, out_shape=(vmem(rows_shape, BF16), vmem(cache_shape...  60.4 us
    pallas_call x1, Pallas kernels, body(): pl.pallas_call(hand_out, out_shape=tuple((jax.ShapeDtypeStruct(shape, BF1...  2.17 us

commit v1 on v0

--- a/solution.py
+++ b/solution.py
@@ -191,23 +191,22 @@
     def start_of(dx, low):
         return away(dx, x, -sign) * 4 + owner_low(low) * 2
 
-    def turn_keys(low):
+    def turn(low):
         wait_for(keys_line[low], line_recv.at[low])
         pack_keys(low)
-        for dx, dy in PLANE[low]:
-            send_plane(keys_packed, dx, dy, keys_land.at[here], keys_send, keys_recv)
-
-    def turn_values(low):
-        for dx, low in ARRIVALS[low]:
+        chips = list(PLANE[low])
+        for dx, _ in ARRIVALS[low]:
             group = group_of(dx, low)
             wait_for(values_mid.at[:, pl.ds(0, 2)], mid_recv.at[group])
-            pair = pl.ds(start_of(dx, low), 2)
+            pair = pl.ds(away(dx, x, -sign) * 4 + owner_low(low) * 2, 2)
             for dz in (1, 3, 2):
                 to_z = away(dz, z, sign)
                 remote(
                     values_mid.at[to_z, pair], values_land.at[z, pair],
                     values_send, values_recv.at[group], (s, in_line(to_z), b),
                 ).start()
+                if dz != 3 and chips:
+                    send_plane(keys_packed, *chips.pop(0), keys_land.at[here], keys_send, keys_recv)
 
     for n, part in enumerate((query_all, fresh_all.at[0], fresh_all.at[1])):
         wait_for(part, small_recv.at[n])
@@ -265,8 +264,7 @@
         return carry
 
     lax.fori_loop(0, 4, attend_section, 0)
-    turn_keys(1)
-    turn_values(1)
+    turn(1)
     lax.fori_loop(4, 8, attend_section, 0)
 
     def send_rows(to_s, to_b):
@@ -283,8 +281,7 @@
     lax.fori_loop(1, 8, send_rows_step, 0)
     send_rows(s, other)
     pltpu.make_async_copy(rows_send.at[s, b], rows_land.at[s, b], rows_recv_sem).start()
-    turn_keys(0)
-    turn_values(0)
+    turn(0)
 
     slots = [slot_order[s * 4 + k] for k in range(4)]
     lives = [lengths[slot] for slot in slots]

time: 63.3 us -> 63.3 us (level)
  no operation moved by 1% of the time
where the time goes in v1:
time: 63.3 us; the launch traced here: 63.2 us
  Pallas kernels  62.6 us (99%)
  between operations  0.64 us (1%)
    pallas_call x1, Pallas kernels, body(): pl.pallas_call(relay, out_shape=(vmem(rows_shape, BF16), vmem(cache_shape...  60.4 us
    pallas_call x1, Pallas kernels, body(): pl.pallas_call(hand_out, out_shape=tuple((jax.ShapeDtypeStruct(shape, BF1...  2.17 us

profile of v1, /device:TPU:1, one launch (start us, length us, event | category | flops | bytes accessed | tf_op | source)
XLA Modules:
  0.0 63.2 jit_solution(17629310875613086852)
XLA Ops:
  0.6 60.4 %relay.1 = (bf16[2,8,4,512]{3,2,1,0:T(4,128)(2,1)S(1)}, bf16[8,4,32,1024]{3,2,1,0:T(8,128)(2,1)S(1)}, bf16[8,4,32,1024]{3,2,1,0:T(8,128)(2,1)S(1)}) custom-call(s32[32]{0:T(128)} %slot_order_hbm.1, s32[32]{0:T(128)} %lengths_hbm.1, bf16[16,4,2,2,32,128]{5,4,3,2,1,0:T(8,128)(2,1)} %bitcast.2, bf16[16,4,2,2,32,128]{5,4,3,2,1,0:T(8,128)(2,1)} %bitcast.3, ...), custom_call_target="tpu_custom_call" | custom-call | tf_op jit(solution)/shard_map/relay/pallas_call | solution.py:393
  61.1 2.2 %hand_out.1 = (bf16[2,8,4,512]{3,2,1,0:T(4,128)(2,1)}, bf16[8,4,32,1024]{3,2,1,0:T(8,128)(2,1)}, bf16[8,4,32,1024]{3,2,1,0:T(8,128)(2,1)}) custom-call(bf16[2,8,4,512]{3,2,1,0:T(4,128)(2,1)S(1)} %get-tuple-element.6.attention, bf16[8,4,32,1024]{3,2,1,0:T(8,128)(2,1)S(1)} %get-tuple-element.7.keys, bf16[8,4,32,1024]{3,2,1,0:T(8,128)(2,1)S(1)} %get-tuple-element.8.values), custom_call_target="tpu_custom_call" | custom-call | tf_op jit(solution)/shard_map/hand_out/pallas_call | solution.py:415

commit v2 on v1

--- a/solution.py
+++ b/solution.py
@@ -26,11 +26,11 @@
 
 
 def relay(
-    slot_order_hbm, lengths_hbm, keys, values, queries, new_keys, new_values,
+    slot_order_hbm, lengths_hbm, keys, values, keys_flat, values_flat, queries, new_keys, new_values,
     attention, keys_cache, values_cache,
-    full, keys_line, values_chip, keys_packed, values_packed, keys_land, values_mid, values_land,
-    fresh_rows, query_all, query_rows, fresh_all, rows_send, rows_land,
-    slot_order, lengths,
+    key_columns, value_rows, keys_line, values_chip, keys_packed, values_packed, keys_land, values_mid, values_land,
+    fresh_rows, query_all, query_rows, fresh_all, result, rows_send, rows_land,
+    slot_order, lengths, slot_of,
     scalar_sem, full_sem, fresh_sem, line_send, line_recv, chip_send, chip_recv,
     keys_send, keys_recv, mid_send, mid_recv, values_send, values_recv,
     small_send, small_recv, rows_send_sem, rows_recv_sem,
@@ -87,7 +87,11 @@
         pltpu.make_async_copy(slot_order_hbm, slot_order, scalar_sem.at[0]),
         pltpu.make_async_copy(lengths_hbm, lengths, scalar_sem.at[1]),
     ]
-    whole = [pltpu.make_async_copy(src, full.at[n], full_sem.at[n]) for n, src in enumerate((keys, values))]
+    whole = [
+        pltpu.make_async_copy(keys_flat.at[at], key_columns.at[:, pl.ds(at * HD, HD)], full_sem.at[0])
+        for at in range(16)
+    ]
+    whole.append(pltpu.make_async_copy(values_flat, value_rows, full_sem.at[1]))
     fresh = [
         pltpu.make_async_copy(src, fresh_rows.at[n], fresh_sem.at[n])
         for n, src in enumerate((new_keys, new_values))
@@ -210,62 +214,95 @@
 
     for n, part in enumerate((query_all, fresh_all.at[0], fresh_all.at[1])):
         wait_for(part, small_recv.at[n])
-    whole[0].wait()
-    whole[1].wait()
-
-    later = lax.rem(lax.div(lax.broadcasted_iota(jnp.int32, (16, 1), 0), 4), 2) == 1
-    column = lax.broadcasted_iota(jnp.int32, (16, 512), 1)
-    scale = HD ** -0.5
-
-    def attend(at_s, at_k):
-        slot = slot_order[at_s * 4 + at_k]
-        prompt = slot - b * 16
-        inside = jnp.logical_and(prompt >= 0, prompt < 16)
-        prompt = jnp.clip(prompt, 0, 15)
-        live = lengths[slot]
-        qf = query_rows[at_k]
-        k0, k1, v0, v1 = (
-            fresh_all[n, at_s, t].astype(F32)[at_k : at_k + 1] for n in range(2) for t in range(2)
-        )
-        k = full[0, prompt].reshape(512, HD)
-        v = full[1, prompt].reshape(512, HD)
-        scores = lax.dot_general(
-            qf.astype(BF16), k, (((1,), (1,)), ((), ())), preferred_element_type=F32
-        ) * scale
-        n0 = jnp.sum(qf * k0, axis=1, keepdims=True) * scale
-        n1 = jnp.sum(qf * k1, axis=1, keepdims=True) * scale
-        kept = column < live
-        scores = jnp.where(kept, scores, HIDDEN)
-        n1 = jnp.where(later, n1, HIDDEN)
-        peak = jnp.maximum(jnp.max(scores, axis=1, keepdims=True), jnp.maximum(n0, n1))
-        mass = jnp.where(kept, jnp.exp(scores - peak), 0.0)
-        m0 = jnp.exp(n0 - peak)
-        m1 = jnp.where(later, jnp.exp(n1 - peak), 0.0)
-        total = jnp.sum(mass, axis=1, keepdims=True) + m0 + m1
-        weighted = jnp.dot(mass.astype(BF16), v, preferred_element_type=F32)
-        weighted += m0.astype(BF16).astype(F32) * v0
-        weighted += m1.astype(BF16).astype(F32) * v1
-        return jnp.where(inside, weighted / total, 0.0)
-
-    def attend_section(at_s, carry):
+    wait_for(key_columns, full_sem.at[0])
+    wait_for(value_rows, full_sem.at[1])
+
+    def spread_queries(at_s, carry):
         for t in range(2):
             rows = query_all[at_s, t].astype(F32)
             for g in range(GROUP):
                 row = (g // 4) * 8 + t * 4 + g % 4
                 for k in range(4):
-                    query_rows[k, row : row + 1, :] = rows[k : k + 1, g * HD : g * HD + HD]
+                    query_rows[at_s * 4 + k, row : row + 1, :] = rows[k : k + 1, g * HD : g * HD + HD]
+        return carry
+
+    lax.fori_loop(0, 8, spread_queries, 0)
+
+    def find_slot(at, carry):
+        found = jnp.int32(0)
+        for slot in range(32):
+            found = jnp.where(slot_order[slot] == b * 16 + at, slot, found)
+        slot_of[at] = found
+        return carry
+
+    lax.fori_loop(0, 16, find_slot, 0)
+
+    lane = lax.broadcasted_iota(jnp.int32, (1, HD), 1)
+    lane_prompt = lax.div(lane, 16)
+    lane_later = lax.rem(lax.div(lane, 4), 2) == 1
+    block_lane = lax.div(lax.broadcasted_iota(jnp.int32, (HD, HD), 1), 16)
+    row4 = lax.broadcasted_iota(jnp.int32, (4, HD), 0)
+    row512 = lax.broadcasted_iota(jnp.int32, (512, HD), 0)
+    scale = HD ** -0.5
+
+    def attend(first):
+        slots = [slot_of[first + p] for p in range(8)]
+        live = jnp.zeros((1, HD), jnp.int32)
+        for p in range(8):
+            live = jnp.where(lane_prompt == p, lengths[first + p + b * 16], live)
+
+        def fresh_row(n, t, slot):
+            rows = fresh_all[n, lax.div(slot, 4), t].astype(F32)
+            return jnp.sum(jnp.where(row4 == lax.rem(slot, 4), rows, 0.0), axis=0, keepdims=True)
+
+        questions = jnp.concatenate([query_rows[slot] for slot in slots], axis=0).T
+        diagonal = jnp.concatenate(
+            [jnp.where(block_lane == p, questions, 0.0) for p in range(8)], axis=0
+        ).astype(BF16)
+        fresh_keys = jnp.concatenate(
+            [
+                jnp.concatenate([fresh_row(0, 0, slot), fresh_row(0, 1, slot), jnp.zeros((14, HD), F32)], axis=0)
+                for slot in slots
+            ],
+            axis=1,
+        ).astype(BF16)
+        scores = jnp.dot(
+            key_columns[:, first * HD : (first + 8) * HD], diagonal, preferred_element_type=F32
+        ) * scale
+        fresh_scores = jnp.dot(fresh_keys, diagonal, preferred_element_type=F32) * scale
+        kept = row512 < live
+        scores = jnp.where(kept, scores, HIDDEN)
+        n0 = fresh_scores[0:1]
+        n1 = jnp.where(lane_later, fresh_scores[1:2], HIDDEN)
+        peak = jnp.maximum(jnp.max(scores, axis=0, keepdims=True), jnp.maximum(n0, n1))
+        mass = jnp.where(kept, jnp.exp(scores - peak), 0.0)
+        m0 = jnp.exp(n0 - peak)
+        m1 = jnp.where(lane_later, jnp.exp(n1 - peak), 0.0)
+        total = jnp.sum(mass, axis=0, keepdims=True) + m0 + m1
+        weights = mass.T.astype(BF16)
+        m0, m1 = (m.astype(BF16).astype(F32) for m in (m0, m1))
+        sides = jnp.concatenate([total, m0, m1, jnp.zeros((HD - 3, HD), F32)], axis=0).T
+        for p, slot in enumerate(slots):
+            cut = slice(p * 16, p * 16 + 16)
+            weighted = jnp.dot(weights[cut], value_rows[first + p], preferred_element_type=F32)
+            weighted += sides[cut, 1:2] * fresh_row(1, 0, slot)
+            weighted += sides[cut, 2:3] * fresh_row(1, 1, slot)
+            result[first + p] = weighted / sides[cut, 0:1]
+
+    attend(0)
+    attend(8)
+
+    def hand_rows(at_s, carry):
         for pair in range(2):
-            first, second = attend(at_s, pair * 2), attend(at_s, pair * 2 + 1)
+            first, second = (
+                result[jnp.clip(slot_order[at_s * 4 + pair * 2 + n] - b * 16, 0, 15)] for n in range(2)
+            )
             for to_b in range(2):
                 cut = slice(to_b * 8, to_b * 8 + 8)
-                rows_send[at_s, to_b, pair] = jnp.concatenate(
-                    (first[cut], second[cut]), axis=0
-                ).astype(BF16)
-        return carry
-
-    lax.fori_loop(0, 4, attend_section, 0)
-    turn(1)
-    lax.fori_loop(4, 8, attend_section, 0)
+                rows_send[at_s, to_b, pair] = jnp.concatenate((first[cut], second[cut]), axis=0).astype(BF16)
+        return carry
+
+    lax.fori_loop(0, 8, hand_rows, 0)
 
     def send_rows(to_s, to_b):
         remote(
@@ -281,6 +318,7 @@
     lax.fori_loop(1, 8, send_rows_step, 0)
     send_rows(s, other)
     pltpu.make_async_copy(rows_send.at[s, b], rows_land.at[s, b], rows_recv_sem).start()
+    turn(1)
     turn(0)
 
     slots = [slot_order[s * 4 + k] for k in range(4)]
@@ -353,11 +391,8 @@
             for dz in (1, 3, 2):
                 settle_values(values_land, from_x, low, away(dz, z, -sign))
 
-    half = full.at[0, :, pl.ds(0, 2)]
-    wait_for(half, chip_send)
-    wait_for(half, line_send)
-    wait_for(full.at[0, :, pl.ds(2, 1)], line_send)
-    wait_for(full.at[0, :, pl.ds(3, 1), pl.ds(0, 1)], line_send)
+    wait_for(value_rows.at[pl.ds(0, 8)], chip_send)
+    wait_for(value_rows.at[pl.ds(0, 14)], line_send)
     for n, part in enumerate((query_all, fresh_all.at[0], fresh_all.at[1])):
         wait_for(part.at[pl.ds(0, 7)], small_send.at[n])
     wait_for(values_packed.at[pl.ds(0, 15)], mid_send)
@@ -380,6 +415,7 @@
 def body(keys_prefill, values_prefill, lengths, slot_order, queries, new_keys, new_values):
     keys = keys_prefill.reshape(16, 4, 2, 2, BLOCK, HD)
     values = values_prefill.reshape(16, 4, 2, 2, BLOCK, HD)
+    flat = (keys_prefill.reshape(16, 512, HD), values_prefill.reshape(16, 512, HD))
     any_spec = pl.BlockSpec(memory_space=pl.ANY)
     hbm_spec = pl.BlockSpec(memory_space=pltpu.HBM)
     vmem_spec = pl.BlockSpec(memory_space=pltpu.VMEM)
@@ -393,16 +429,16 @@
     held = pl.pallas_call(
         relay,
         out_shape=(vmem(rows_shape, BF16), vmem(cache_shape, BF16), vmem(cache_shape, BF16)),
-        in_specs=[hbm_spec] * 7,
+        in_specs=[hbm_spec] * 9,
         out_specs=(vmem_spec,) * 3,
         scratch_shapes=[
-            vmem((2, 16, 4, 2, 2, BLOCK, HD), BF16),
+            vmem((512, 16 * HD), BF16), vmem((16, 512, HD), BF16),
             [vmem((4, 32, BLOCK, HD), BF16)] * 2, [vmem((32, 4, BLOCK, HD), BF16)] * 2,
             plane, plane, plane, line, line,
-            vmem((2, 2, 8, 4, KVH * HD), BF16), vmem((8, 2, 4, GROUP * HD), BF16), vmem((4, 16, HD), F32),
-            vmem((2, 8, 2, 4, HD), BF16),
+            vmem((2, 2, 8, 4, KVH * HD), BF16), vmem((8, 2, 4, GROUP * HD), BF16), vmem((32, 16, HD), F32),
+            vmem((2, 8, 2, 4, HD), BF16), vmem((16, 16, HD), F32),
             vmem((8, 2, 2, 16, HD), BF16), vmem((8, 2, 2, 16, HD), BF16),
-            pltpu.SMEM((32,), jnp.int32), pltpu.SMEM((32,), jnp.int32),
+            pltpu.SMEM((32,), jnp.int32), pltpu.SMEM((32,), jnp.int32), pltpu.SMEM((16,), jnp.int32),
             dma((2,)), dma((2,)), dma((2,)), dma, dma((2,)), dma, dma((2,)),
             dma, dma((8,)), dma, dma((8,)), dma, dma((8,)),
             dma((3,)), dma((3,)), dma, dma,
@@ -411,7 +447,7 @@
             collective_id=0, has_side_effects=True, vmem_limit_bytes=48 * 2**20
         ),
         name="relay",
-    )(*(in_hbm(x) for x in (slot_order, lengths, keys, values, queries, new_keys, new_values)))
+    )(*(in_hbm(x) for x in (slot_order, lengths, keys, values, *flat, queries, new_keys, new_values)))
     return pl.pallas_call(
         hand_out,
         out_shape=tuple(jax.ShapeDtypeStruct(shape, BF16) for shape in (rows_shape, cache_shape, cache_shape)),

time: 63.3 us -> 63.3 us (level)
  no operation moved by 1% of the time
where the time goes in v2:
time: 63.3 us; the launch traced here: 63.2 us
  Pallas kernels  62.6 us (99%)
  between operations  0.64 us (1%)
    pallas_call x1, Pallas kernels, body(): pl.pallas_call(relay, out_shape=(vmem(rows_shape, BF16), vmem(cache_shape...  60.4 us
    pallas_call x1, Pallas kernels, body(): pl.pallas_call(hand_out, out_shape=tuple((jax.ShapeDtypeStruct(shape, BF1...  2.17 us

profile of v2, /device:TPU:1, one launch (start us, length us, event | category | flops | bytes accessed | tf_op | source)
XLA Modules:
  0.0 63.2 jit_solution(6036671667678723241)
XLA Ops:
  0.6 60.4 %relay.1 = (bf16[2,8,4,512]{3,2,1,0:T(4,128)(2,1)S(1)}, bf16[8,4,32,1024]{3,2,1,0:T(8,128)(2,1)S(1)}, bf16[8,4,32,1024]{3,2,1,0:T(8,128)(2,1)S(1)}) custom-call(s32[32]{0:T(128)} %slot_order_hbm.1, s32[32]{0:T(128)} %lengths_hbm.1, bf16[16,4,2,2,32,128]{5,4,3,2,1,0:T(8,128)(2,1)} %bitcast.4, bf16[16,4,2,2,32,128]{5,4,3,2,1,0:T(8,128)(2,1)} %bitcast.6, ...), custom_call_target="tpu_custom_call" | custom-call | tf_op jit(solution)/shard_map/relay/pallas_call | solution.py:429
  61.0 2.2 %hand_out.1 = (bf16[2,8,4,512]{3,2,1,0:T(4,128)(2,1)}, bf16[8,4,32,1024]{3,2,1,0:T(8,128)(2,1)}, bf16[8,4,32,1024]{3,2,1,0:T(8,128)(2,1)}) custom-call(bf16[2,8,4,512]{3,2,1,0:T(4,128)(2,1)S(1)} %get-tuple-element.6.attention, bf16[8,4,32,1024]{3,2,1,0:T(8,128)(2,1)S(1)} %get-tuple-element.7.keys, bf16[8,4,32,1024]{3,2,1,0:T(8,128)(2,1)S(1)} %get-tuple-element.8.values), custom_call_target="tpu_custom_call" | custom-call | tf_op jit(solution)/shard_map/hand_out/pallas_call | solution.py:451
